TPU v7x, 512 devices: a whole 4x8x8 slice. The times are simulated.
512 devices in a mesh: rep: 64 (over y, x, z_lo), ctx: 8 (over z_hi, core).
Axes of the slice: x: 4, y: 8, z: 8 (z_hi: 4, z_lo: 2; z = z_hi * 2 + z_lo), core: 2. Of those that a mesh axis runs over, the one named last changes fastest.
Arguments:
- hidden: bfloat16 [64, 1024, 3584], P('rep', 'ctx'), may hold values from -6 to 6
- queries: bfloat16 [64, 1024, 2048], P('rep', 'ctx'), may hold values from -16 to 16
- values: bfloat16 [64, 1024, 1024], P('rep', 'ctx'), may hold values from -6 to 6
- cotangent: bfloat16 [64, 1024, 2048], P('rep', 'ctx'), may hold values from -6 to 6
- key_weight: bfloat16 [64, 3584, 1024], P('rep', None, 'ctx'), may hold values from -0.09375 to 0.09375
- doc_ids: int32 [64, 1024], P('rep', 'ctx'), may hold values from 0 to 3, never falling along the last dimension, each value on 1 to 512 neighbouring positions
- round_index: int32 [3], replicated, may hold values from 0 to 5
Outputs:
- averaged: bfloat16 [64, 3584, 1024], P('rep', None, 'ctx')
- gradient: bfloat16 [64, 3584, 1024], P('rep', None, 'ctx')
Inputs may be any that keep to these rules, and one draw needn't show every extreme that they name: `doc_ids`: document numbers never fall along a replica's positions; each document holds at most 512 positions and one holds exactly that many. `round_index`: the same rounds for every replica.
All inputs are finite; a program needn't handle non-finite values.
Results may differ from a plain program's by a relative error of at most 0.019.
Values may be sent and summed in bfloat16 or wider, within the bound.
A program may use at most 64 MiB of HBM per device.

v0:
```python
from functools import partial

import jax
import jax.numpy as jnp
from jax import lax
from jax.experimental import pallas as pl
from jax.experimental.pallas import tpu as pltpu
from jax.sharding import PartitionSpec as P

MESH = pl.DeviceIdType.MESH

HDIM = 256
HEADS = 8
KVH = 4
GOSSIP = 3
N_CTX = 8
CHIPS = 4
ROWS = 128
CHUNKS = 4

softcap = 50.0
step_size = 0.0005


def swapped(x, axis, apart):
    return lax.ppermute(x, axis, [(i, i ^ 1 << apart) for i in range(lax.axis_size(axis))])


def round_partner(payload, round_number, rounds):
    branches = [partial(swapped, axis="rep", apart=level_bit) for level_bit in range(rounds)]
    return lax.switch(round_number, branches, payload)


def nt(a, b):
    return lax.dot_general(a, b, (((1,), (1,)), ((), ())), preferred_element_type=jnp.float32)


def gradient_kernel(
    hid, qry, val, cot, wgt, docs, grad, stepped,
    hall, qall, call, vall, dall, wown, kbuf, dkacc, dksend, dkrecv, dkown,
    local, h_recv, h_send, q_recv, q_send, c_recv, c_send, v_recv, v_send, d_recv, d_send,
    k_recv, k_send, g_recv, g_send,
):
    me = lax.axis_index("ctx")
    chip = me // 2
    core = lax.rem(me, 2)
    sib = chip * 2 + (1 - core)
    up_chip = lax.rem(chip + 1, CHIPS)
    dn_chip = lax.rem(chip + 3, CHIPS)
    opp_chip = lax.rem(chip + 2, CHIPS)
    up = up_chip * 2 + core
    dn = dn_chip * 2 + core
    opp = opp_chip * 2 + core
    rows_of = ROWS // CHUNKS

    def send(src, dst, ssem, rsem, dev):
        return pltpu.make_async_remote_copy(
            src_ref=src, dst_ref=dst, send_sem=ssem, recv_sem=rsem,
            device_id={"ctx": dev}, device_id_type=MESH,
        )

    barrier = pltpu.get_barrier_semaphore()
    for other in range(1, N_CTX):
        pl.semaphore_signal(
            barrier, inc=1, device_id={"ctx": lax.rem(me + other, N_CTX)}, device_id_type=MESH
        )

    head = pl.ds(pl.multiple_of(me * HDIM, HDIM), HDIM)
    kv_head = pl.ds(pl.multiple_of(chip * HDIM, HDIM), HDIM)
    own_half = pl.ds(pl.multiple_of(core * 128, 128), 128)
    sib_half = pl.ds(pl.multiple_of((1 - core) * 128, 128), 128)
    local_copies = [
        pltpu.make_async_copy(hid, hall.at[me], local.at[0]),
        pltpu.make_async_copy(wgt, wown, local.at[1]),
        pltpu.make_async_copy(qry.at[:, head], qall.at[me], local.at[2]),
        pltpu.make_async_copy(cot.at[:, head], call.at[me], local.at[3]),
        pltpu.make_async_copy(val.at[:, kv_head], vall.at[me], local.at[4]),
    ]
    for copy in local_copies:
        copy.start()
    pl.semaphore_wait(barrier, N_CTX - 1)

    started = []

    def go(copy):
        copy.start()
        started.append(copy)

    def piece(k):
        return pl.ds(k * rows_of, rows_of)

    low = list(range(CHUNKS // 2))
    high = list(range(CHUNKS // 2, CHUNKS))

    def h_to(dev, origin, k, sem, src=None):
        slot = hall.at[origin, piece(k), :]
        go(send(slot if src is None else src, slot, h_send.at[sem], h_recv.at[origin, k], dev))

    def h_wait(origin, k):
        slot = hall.at[origin, piece(k), :]
        send(slot, slot, h_send.at[0], h_recv.at[origin, k], sib).wait_recv()

    for a, b in zip(low + high, high + low):
        h_to(up, me, a, a, hid.at[piece(a), :])
        h_to(dn, me, b, CHUNKS + b, hid.at[piece(b), :])
    for k in range(CHUNKS):
        h_to(sib, me, k, 2 * CHUNKS + k, hid.at[piece(k), :])
    go_docs = []
    for other in range(1, N_CTX):
        dev = lax.rem(me + other, N_CTX)
        go(send(docs, dall.at[me], d_send.at[other], d_recv.at[me], dev))
    dall[me] = docs[...]

    sem = 3 * CHUNKS
    for a, b in zip(low, high):
        h_wait(dn, a)
        h_to(up, dn, a, sem, None)
        h_to(sib, dn, a, sem + 1, None)
        h_wait(up, b)
        h_to(dn, up, b, sem + 2, None)
        h_to(sib, up, b, sem + 3, None)
        sem += 4

    for i, (far_chip, far) in enumerate(((up_chip, up), (dn_chip, dn), (opp_chip, opp))):
        for j in range(2):
            dev = far_chip * 2 + j
            feats = pl.ds(pl.multiple_of(dev * HDIM, HDIM), HDIM)
            go(send(qry.at[:, feats], qall.at[me], q_send.at[2 * i + j], q_recv.at[me], dev))
            go(send(cot.at[:, feats], call.at[me], c_send.at[2 * i + j], c_recv.at[me], dev))
        feats = pl.ds(pl.multiple_of(far_chip * HDIM, HDIM), HDIM)
        go(send(val.at[:, feats], vall.at[me], v_send.at[i], v_recv.at[me], far))
    sib_feats = pl.ds(pl.multiple_of(sib * HDIM, HDIM), HDIM)
    go(send(qry.at[:, sib_feats], qall.at[me], q_send.at[6], q_recv.at[me], sib))
    go(send(cot.at[:, sib_feats], call.at[me], c_send.at[6], c_recv.at[me], sib))
    go(send(val.at[:, kv_head], vall.at[me], v_send.at[3], v_recv.at[me], sib))

    for copy in local_copies:
        copy.wait()

    def project(p):
        block = hall[pl.ds(2 * p, 2)].reshape(2 * ROWS, hall.shape[2])
        out = jnp.dot(block, wown[...], preferred_element_type=jnp.float32)
        rows = pl.ds(pl.multiple_of(p * 2 * ROWS, 2 * ROWS), 2 * ROWS)
        kbuf[rows, own_half] = out.astype(jnp.bfloat16)
        go(send(kbuf.at[rows, own_half], kbuf.at[rows, own_half], k_send.at[p], k_recv.at[p], sib))

    for k in range(CHUNKS):
        h_wait(sib, k)
    project(chip)

    for a, b in zip(high, low):
        h_wait(dn, a)
        h_to(sib, dn, a, sem, None)
        h_wait(up, b)
        h_to(sib, up, b, sem + 1, None)
        sem += 2
    for k in range(CHUNKS):
        h_wait(up_chip * 2 + 1 - core, k)
    project(up_chip)
    for k in range(CHUNKS):
        h_wait(dn_chip * 2 + 1 - core, k)
    project(dn_chip)
    for a, b in zip(low, high):
        h_wait(opp, a)
        h_to(sib, opp, a, sem, None)
        h_wait(opp, b)
        h_to(sib, opp, b, sem + 1, None)
        sem += 2
    for k in range(CHUNKS):
        h_wait(opp_chip * 2 + 1 - core, k)
    project(opp_chip)

    for i, far in enumerate((up, dn, opp)):
        send(vall.at[far], vall.at[far], v_send.at[0], v_recv.at[far], sib).wait_recv()
        go(send(vall.at[far], vall.at[far], v_send.at[4 + i], v_recv.at[far], sib))
    for other in range(1, N_CTX):
        src = lax.rem(me + other, N_CTX)
        send(qall.at[src], qall.at[src], q_send.at[0], q_recv.at[src], sib).wait_recv()
        send(call.at[src], call.at[src], c_send.at[0], c_recv.at[src], sib).wait_recv()
        send(docs, dall.at[src], d_send.at[0], d_recv.at[src], sib).wait_recv()
    for p in (chip, up_chip, dn_chip, opp_chip):
        src = 2 * p + 1 - core
        send(vall.at[src], vall.at[src], v_send.at[0], v_recv.at[src], sib).wait_recv()
        rows = pl.ds(pl.multiple_of(p * 2 * ROWS, 2 * ROWS), 2 * ROWS)
        half = kbuf.at[rows, sib_half]
        send(half, half, k_send.at[0], k_recv.at[p], sib).wait_recv()

    doc_rows = [dall[s] for s in range(N_CTX)]
    starts = [jnp.zeros(row.shape, jnp.float32) for row in doc_rows]
    for v in range(3):
        total = jnp.zeros((1, 1), jnp.float32)
        for row in doc_rows:
            total = total + jnp.sum(jnp.where(row == v, 1.0, 0.0), axis=1, keepdims=True)
        starts = [s + jnp.where(row > v, total, 0.0) for s, row in zip(starts, doc_rows)]

    dkacc[...] = jnp.zeros_like(dkacc)
    block = 2 * ROWS
    for p in range(CHIPS):
        first = max(p - 2, 0)
        keys = (p + 1 - first) * block
        rows = pl.ds(first * block, keys)
        q = qall[2 * p : 2 * p + 2].reshape(block, HDIM)
        c = call[2 * p : 2 * p + 2].reshape(block, HDIM)
        v = vall[2 * first : 2 * p + 2].reshape(keys, HDIM)
        start = jnp.concatenate([starts[2 * p], starts[2 * p + 1]], axis=1).astype(jnp.int32)
        t = jnp.tanh(nt(kbuf[rows, :], q) * (1.0 / (HDIM**0.5 * softcap)))
        key_pos = first * block + lax.broadcasted_iota(jnp.int32, (keys, block), 0)
        query_pos = p * block + lax.broadcasted_iota(jnp.int32, (keys, block), 1)
        allowed = (key_pos <= query_pos) & (key_pos >= start)
        e = jnp.where(allowed, jnp.exp(softcap * t), 0.0)
        prob_grad = nt(v, c)
        norm = 1.0 / jnp.sum(e, axis=0, keepdims=True)
        row_dot = jnp.sum(e * prob_grad, axis=0, keepdims=True) * norm
        score_grad = (e * norm) * (prob_grad - row_dot) * (1.0 - t * t)
        dkacc[rows, :] += jnp.dot(
            score_grad.astype(jnp.bfloat16), q, preferred_element_type=jnp.float32
        )

    scale = 1.0 / HDIM**0.5
    dksend[...] = (dkacc[:, sib_half] * scale).astype(jnp.bfloat16)
    swap = send(dksend, dkrecv, g_send.at[0], g_recv.at[0], sib)
    go(swap)
    swap.wait_recv()
    dk = dkacc[:, own_half] * scale + dkrecv[...].astype(jnp.float32)
    dkown[...] = dk.T.astype(jnp.bfloat16)

    width = 512

    @pl.loop(0, grad.shape[0] // width)
    def _(i):
        cols = pl.ds(pl.multiple_of(i * width, width), width)
        h = hall[:, :, cols].reshape(N_CTX * ROWS, width)
        g = jnp.dot(dkown[...], h, preferred_element_type=jnp.float32).T
        grad[cols, :] = g.astype(jnp.bfloat16)
        stepped[cols, :] = (wown[cols, :].astype(jnp.float32) - step_size * g).astype(jnp.bfloat16)

    for copy in started:
        copy.wait_send()


def local_gradient(hidden, queries, values, cotangent, key_weight, doc_ids):
    depth = hidden.shape[1]
    dma = pltpu.SemaphoreType.DMA
    bf16, f32 = jnp.bfloat16, jnp.float32
    any_spec = pl.BlockSpec(memory_space=pl.ANY)
    vmem = pl.BlockSpec(memory_space=pltpu.VMEM)
    seq = N_CTX * ROWS
    return pl.pallas_call(
        gradient_kernel,
        out_shape=[jax.ShapeDtypeStruct((depth, 128), bf16)] * 2,
        in_specs=[any_spec] * 5 + [vmem],
        out_specs=[vmem] * 2,
        scratch_shapes=[
            pltpu.VMEM((N_CTX, ROWS, depth), bf16),
            pltpu.VMEM((N_CTX, ROWS, HDIM), bf16),
            pltpu.VMEM((N_CTX, ROWS, HDIM), bf16),
            pltpu.VMEM((N_CTX, ROWS, HDIM), bf16),
            pltpu.VMEM((N_CTX, 1, ROWS), jnp.int32),
            pltpu.VMEM((depth, 128), bf16),
            pltpu.VMEM((seq, HDIM), bf16),
            pltpu.VMEM((seq, HDIM), f32),
            pltpu.VMEM((seq, 128), bf16),
            pltpu.VMEM((seq, 128), bf16),
            pltpu.VMEM((128, seq), bf16),
            dma((5,)),
            dma((N_CTX, CHUNKS)),
            dma((7 * CHUNKS,)),
            dma((N_CTX,)),
            dma((7,)),
            dma((N_CTX,)),
            dma((7,)),
            dma((N_CTX,)),
            dma((7,)),
            dma((N_CTX,)),
            dma((N_CTX,)),
            dma((CHIPS,)),
            dma((CHIPS,)),
            dma((1,)),
            dma((1,)),
        ],
        compiler_params=pltpu.CompilerParams(
            collective_id=0, has_side_effects=True, vmem_limit_bytes=48 * 1024 * 1024
        ),
        name="gradient",
    )(hidden, queries, values, cotangent, key_weight, doc_ids)


def on_device(hidden, queries, values, cotangent, key_weight, doc_ids, round_index):
    rounds = lax.axis_size("rep").bit_length() - 1
    gradient, averaged = local_gradient(
        hidden[0], queries[0], values[0], cotangent[0], key_weight[0], doc_ids
    )
    for turn in range(GOSSIP):
        partner = round_partner(averaged, round_index[turn], rounds)
        averaged = (0.5 * (averaged.astype(jnp.float32) + partner.astype(jnp.float32))).astype(
            jnp.bfloat16
        )
    return (averaged[None], gradient[None])


def solution(mesh):
    return jax.shard_map(
        on_device,
        mesh=mesh,
        in_specs=(
            P("rep", "ctx", None),
            P("rep", "ctx", None),
            P("rep", "ctx", None),
            P("rep", "ctx", None),
            P("rep", None, "ctx"),
            P("rep", "ctx"),
            P(),
        ),
        out_specs=(P("rep", None, "ctx"), P("rep", None, "ctx")),
        check_vma=False,
    )
```

profile of v0, /device:TPU:60, one launch (start us, length us, event | category | flops | bytes accessed | tf_op | source)
XLA Modules:
  0.0 240.2 jit_solution(17017096839583819880)
XLA Ops:
  0.6 1.4 fusion.1
  4.1 0.0 copy-start
  4.1 1.2 copy-done
  5.2 0.0 copy-start.1
  5.2 1.2 copy-done.1
  6.4 0.0 copy-start.2
  6.4 1.0 copy-done.2
  7.5 1.0 copy-done.3
  8.5 0.9 copy-done.4
  9.5 0.7 copy-done.5
  10.1 78.5 %gradient.1 = (bf16[3584,128]{1,0:T(8,128)(2,1)S(1)}, bf16[3584,128]{1,0:T(8,128)(2,1)S(1)}) custom-call(bf16[128,3584]{1,0:T(8,128)(2,1)S(1)} %bitcast.12, bf16[128,2048]{1,0:T(8,128)(2,1)S(1)} %bitcast.14, bf16[128,1024]{1,0:T(8,128)(2,1)S(1)} %bitcast.16, bf16[128,2048]{1,0:T(8,128)(2,1)S(1)} %bitcast.15, bf16[3584,128]{1,0:T(8,128)(2,1)S(1)} %bitcast.13, ...), custom_call_target="tpu_custom_call" | custom-call | tf_op jit(solution)/shard_map/gradient/pallas_call | solution.py:248
  88.6 44.5 %conditional.12 = (bf16[3584,128]{1,0:T(8,128)(2,1)}) conditional(s32[]{:T(128)} %bitcast.5, bf16[3584,128]{1,0:T(8,128)(2,1)S(1)} %get-tuple-element.61, bf16[3584,128]{1,0:T(8,128)(2,1)S(1)} %get-tuple-element.61, bf16[3584,128]{1,0:T(8,128)(2,1)S(1)} %get-tuple-element.61, ...), branch_computations={%region_0.0_spmd, %region_1.0_spmd, %region_2.0_spmd, %region_3.0_... | conditional | bytes 3670064
  88.6 4.0 %collective-permute-start.4 = (bf16[3584,128]{1,0:T(8,128)(2,1)S(1)}, bf16[3584,128]{1,0:T(8,128)(2,1)}, u32[]{:S(2)}, u32[]{:S(2)}) collective-permute-start(bf16[3584,128]{1,0:T(8,128)(2,1)S(1)} %param.4), channel_id=1, source_target_pairs={{0,128},{8,136},{16,144},{24,152},{32,160},{40,168},{48,176},{56,1... | collective-permute-start | bytes 2752520 | tf_op jit(solution)/shard_map/cond/branch_4_fun/ppermute | solution.py:26
  92.7 40.4 %collective-permute-done.4 = bf16[3584,128]{1,0:T(8,128)(2,1)} collective-permute-done((bf16[3584,128]{1,0:T(8,128)(2,1)S(1)}, bf16[3584,128]{1,0:T(8,128)(2,1)}, u32[]{:S(2)}, u32[]{:S(2)}) %collective-permute-start.4) | collective-permute-done | bytes 917536 | tf_op jit(solution)/shard_map/cond/branch_4_fun/ppermute | solution.py:26
  133.1 1.5 multiply_convert_fusion.2
  134.5 57.5 %conditional.13 = (bf16[3584,128]{1,0:T(8,128)(2,1)}) conditional(s32[]{:T(128)} %bitcast.6, bf16[3584,128]{1,0:T(8,128)(2,1)S(1)} %multiply_convert_fusion.2, bf16[3584,128]{1,0:T(8,128)(2,1)S(1)} %multiply_convert_fusion.2, bf16[3584,128]{1,0:T(8,128)(2,1)S(1)} %multiply_convert_fusion.2, ...), branch_computations={%region_6.0_spmd, %region_7.0_spmd, %region_8.0_spmd, %region_9.0_... | conditional | bytes 3670064
  134.6 37.7 %collective-permute-start.6 = (bf16[3584,128]{1,0:T(8,128)(2,1)S(1)}, bf16[3584,128]{1,0:T(8,128)(2,1)}, u32[]{:S(2)}, u32[]{:S(2)}) collective-permute-start(bf16[3584,128]{1,0:T(8,128)(2,1)S(1)} %param.6), channel_id=1, source_target_pairs={{0,8},{8,0},{16,24},{24,16},{32,40},{40,32},{48,56},{56,48},{64,72... | collective-permute-start | bytes 2752520 | tf_op jit(solution)/shard_map/cond/branch_0_fun/ppermute | solution.py:26
  172.3 19.8 %collective-permute-done.6 = bf16[3584,128]{1,0:T(8,128)(2,1)} collective-permute-done((bf16[3584,128]{1,0:T(8,128)(2,1)S(1)}, bf16[3584,128]{1,0:T(8,128)(2,1)}, u32[]{:S(2)}, u32[]{:S(2)}) %collective-permute-start.6) | collective-permute-done | bytes 917536 | tf_op jit(solution)/shard_map/cond/branch_0_fun/ppermute | solution.py:26
  192.0 1.5 multiply_convert_fusion.1
  193.5 43.4 %conditional.14 = (bf16[3584,128]{1,0:T(8,128)(2,1)}) conditional(s32[]{:T(128)} %bitcast.7, bf16[3584,128]{1,0:T(8,128)(2,1)S(1)} %multiply_convert_fusion.1, bf16[3584,128]{1,0:T(8,128)(2,1)S(1)} %multiply_convert_fusion.1, bf16[3584,128]{1,0:T(8,128)(2,1)S(1)} %multiply_convert_fusion.1, ...), branch_computations={%region_12.0_spmd, %region_13.0_spmd, %region_14.0_spmd, %region_1... | conditional | bytes 3670064
  193.5 1.9 collective-permute-start.16
  195.5 41.4 %collective-permute-done.16 = bf16[3584,128]{1,0:T(8,128)(2,1)} collective-permute-done((bf16[3584,128]{1,0:T(8,128)(2,1)S(1)}, bf16[3584,128]{1,0:T(8,128)(2,1)}, u32[]{:S(2)}, u32[]{:S(2)}) %collective-permute-start.16) | collective-permute-done | bytes 917536 | tf_op jit(solution)/shard_map/cond/branch_4_fun/ppermute | solution.py:26
  236.9 2.4 fusion
  239.3 0.9 copy.28
  (3 shorter events, 0.0 us)
Async XLA Ops:
  4.1 1.2 copy-start
  5.2 1.2 copy-start.1
  6.4 1.0 copy-start.2
  7.5 1.0 copy-start.3
  8.5 0.9 copy-start.4
  9.5 0.7 copy-start.5
  88.6 44.4 %collective-permute-start.4 = (bf16[3584,128]{1,0:T(8,128)(2,1)S(1)}, bf16[3584,128]{1,0:T(8,128)(2,1)}, u32[]{:S(2)}, u32[]{:S(2)}) collective-permute-start(bf16[3584,128]{1,0:T(8,128)(2,1)S(1)} %param.4), channel_id=1, source_target_pairs={{0,128},{8,136},{16,144},{24,152},{32,160},{40,168},{48,176},{56,1... | collective-permute-start | bytes 2752520 | tf_op jit(solution)/shard_map/cond/branch_4_fun/ppermute | solution.py:26
  134.6 57.5 %collective-permute-start.6 = (bf16[3584,128]{1,0:T(8,128)(2,1)S(1)}, bf16[3584,128]{1,0:T(8,128)(2,1)}, u32[]{:S(2)}, u32[]{:S(2)}) collective-permute-start(bf16[3584,128]{1,0:T(8,128)(2,1)S(1)} %param.6), channel_id=1, source_target_pairs={{0,8},{8,0},{16,24},{24,16},{32,40},{40,32},{48,56},{56,48},{64,72... | collective-permute-start | bytes 2752520 | tf_op jit(solution)/shard_map/cond/branch_0_fun/ppermute | solution.py:26
  193.5 43.3 %collective-permute-start.16 = (bf16[3584,128]{1,0:T(8,128)(2,1)S(1)}, bf16[3584,128]{1,0:T(8,128)(2,1)}, u32[]{:S(2)}, u32[]{:S(2)}) collective-permute-start(bf16[3584,128]{1,0:T(8,128)(2,1)S(1)} %param.16), channel_id=1, source_target_pairs={{0,128},{8,136},{16,144},{24,152},{32,160},{40,168},{48,176},{56,1... | collective-permute-start | bytes 2752520 | tf_op jit(solution)/shard_map/cond/branch_4_fun/ppermute | solution.py:26
where the time goes:
time: 241 us; the launch traced here: 240 us
  waiting for transfers between devices  102 us (42%)
  Pallas kernels  78.5 us (33%)
  starting transfers between devices  43.7 us (18%)
  local copies, waits for them, and re-layouts  8.39 us (3%)
  other arithmetic  5.35 us (2%)
  between operations  2.65 us (1%)
    ppermute x3, waiting for transfers between devices, swapped(): lax.ppermute(x, axis, [(i, i ^ 1 << apart) for i in range(lax.axis_size(a...  102 us
    pallas_call x1, Pallas kernels, local_gradient(): pl.pallas_call(gradient_kernel, out_shape=[jax.ShapeDtypeStruct((depth, 1...  78.5 us
    ppermute x3, starting transfers between devices, swapped(): lax.ppermute(x, axis, [(i, i ^ 1 << apart) for i in range(lax.axis_size(a...  43.7 us
    unnamed x13, local copies, waits for them, and re-layouts  6.96 us
  transfers between devices with their start and end apart: 3, of which 3 were waited for; matrix products, arithmetic and copies ran while one was open for 0% of the time, Pallas kernels for 0%

commit v1 on v0

--- a/solution.py
+++ b/solution.py
@@ -1,3 +1,4 @@
+import itertools
 from functools import partial
 
 import jax
@@ -17,18 +18,144 @@
 CHIPS = 4
 ROWS = 128
 CHUNKS = 4
+RANKS = 6
 
 softcap = 50.0
 step_size = 0.0005
 
 
-def swapped(x, axis, apart):
-    return lax.ppermute(x, axis, [(i, i ^ 1 << apart) for i in range(lax.axis_size(axis))])
-
-
-def round_partner(payload, round_number, rounds):
-    branches = [partial(swapped, axis="rep", apart=level_bit) for level_bit in range(rounds)]
-    return lax.switch(round_number, branches, payload)
+ROUTE = (("z", 1), ("x", 1), ("x", 1), ("y", 1), ("y", 2), ("y", 2))
+PIECES = 7
+
+
+def round_orders(bits):
+    load = {"x": 0.0, "y": 0.0, "z": 0.0}
+    orders = []
+    for _ in range(PIECES):
+        best = None
+        for order in itertools.permutations(bits):
+            after = dict(load)
+            for level, bit in enumerate(order):
+                axis, hops = ROUTE[bit]
+                after[axis] += hops * 0.5**level
+            key = (max(after.values()), sum(after.values()), order)
+            if best is None or key < best[0]:
+                best = (key, order, after)
+        orders.append(best[1])
+        load = best[2]
+    return orders
+
+
+def gossip_kernel(bits, x, out, acc, first, second, third, send_sem, recv_sem):
+    me = lax.axis_index("rep")
+    count = len(bits)
+    landing = (first, second, third)
+    digit = {bit: lax.rem(me // (1 << bit), 2) for bit in bits}
+    partner = {bit: me + (1 - 2 * digit[bit]) * (1 << bit) for bit in bits}
+    barrier = pltpu.get_barrier_semaphore()
+    for bit in bits:
+        pl.semaphore_signal(barrier, inc=1, device_id={"rep": partner[bit]}, device_id_type=MESH)
+    pl.semaphore_wait(barrier, count)
+
+    rows = x.shape[0] // PIECES
+    stages = 2 * count - 1
+    orders = round_orders(bits)
+
+    def region(piece, level):
+        base, size = piece * rows, rows
+        for bit in orders[piece][:level]:
+            size //= 2
+            base = base + digit[bit] * size
+        return base, size
+
+    def at(ref, base, size):
+        start = base if isinstance(base, int) else pl.multiple_of(base, 32)
+        return ref.at[pl.ds(start, size), :]
+
+    def transfer(piece, stage, arriving=False):
+        order = orders[piece]
+        if stage < count - 1:
+            bit = order[stage]
+            base, size = region(piece, stage)
+            half = size // 2
+            src = x if stage == 0 else acc
+            away = base + (1 - digit[bit]) * half
+            sent, dst = at(src, away, half), at(landing[stage], away, half)
+            came = at(landing[stage], base + digit[bit] * half, half)
+        elif stage == count - 1:
+            bit = order[stage]
+            base, size = region(piece, stage)
+            src = x if stage == 0 else acc
+            sent, dst = at(src, base, size), at(landing[stage], base, size)
+            came = dst
+        else:
+            level = stages - 1 - stage
+            bit = order[level]
+            base, size = region(piece, level)
+            half = size // 2
+            sent = at(out, base + digit[bit] * half, half)
+            dst = sent
+            came = at(out, base + (1 - digit[bit]) * half, half)
+
+        return pltpu.make_async_remote_copy(
+            src_ref=sent, dst_ref=came if arriving else dst, send_sem=send_sem.at[piece, stage],
+            recv_sem=recv_sem.at[piece, stage], device_id={"rep": partner[bit]},
+            device_id_type=MESH,
+        )
+
+    def finish(piece, stage):
+        transfer(piece, stage, arriving=True).wait_recv()
+        if stage < count:
+            base, size = region(piece, min(stage + 1, count - 1))
+            own = at(x if stage == 0 else acc, base, size)
+            other = at(landing[stage], base, size)
+            mean = 0.5 * (own[...].astype(jnp.float32) + other[...].astype(jnp.float32))
+            at(out if stage == count - 1 else acc, base, size)[...] = mean.astype(jnp.bfloat16)
+
+    for piece in range(PIECES):
+        transfer(piece, 0).start()
+    for step in range(PIECES + stages - 1):
+        for stage in range(stages - 1, -1, -1):
+            piece = step - stage
+            if 0 <= piece < PIECES:
+                finish(piece, stage)
+                if stage + 1 < stages:
+                    transfer(piece, stage + 1).start()
+    for piece in range(PIECES):
+        for stage in range(stages):
+            transfer(piece, stage).wait_send()
+
+
+def gossip(bits, number):
+    def run(stepped):
+        shape = stepped.shape
+        stages = 2 * len(bits) - 1
+        vmem = pl.BlockSpec(memory_space=pltpu.VMEM)
+        return pl.pallas_call(
+            partial(gossip_kernel, bits),
+            out_shape=jax.ShapeDtypeStruct(shape, jnp.bfloat16),
+            in_specs=[vmem],
+            out_specs=vmem,
+            scratch_shapes=[pltpu.VMEM(shape, jnp.bfloat16)] * 4
+            + [pltpu.SemaphoreType.DMA((PIECES, stages))] * 2,
+            compiler_params=pltpu.CompilerParams(
+                collective_id=number, has_side_effects=True, vmem_limit_bytes=16 * 1024 * 1024
+            ),
+            name="gossip",
+        )(stepped)
+
+    return run
+
+
+def gossip_rounds(stepped, mask):
+    branches = []
+    for case in range(1 << RANKS):
+        bits = tuple(bit for bit in range(RANKS) if case >> bit & 1)
+        if 1 <= len(bits) <= GOSSIP:
+            branches.append(gossip(bits, 1 + case))
+        else:
+            branches.append(lambda kept: kept)
+    return lax.switch(mask, branches, stepped)
 
 
 def nt(a, b):
@@ -36,7 +163,7 @@
 
 
 def gradient_kernel(
-    hid, qry, val, cot, wgt, docs, grad, stepped,
+    hid, qry, val, cot, wgt, docs, rounds, grad, stepped, mask,
     hall, qall, call, vall, dall, wown, kbuf, dkacc, dksend, dkrecv, dkown,
     local, h_recv, h_send, q_recv, q_send, c_recv, c_send, v_recv, v_send, d_recv, d_send,
     k_recv, k_send, g_recv, g_send,
@@ -59,6 +186,7 @@
             device_id={"ctx": dev}, device_id_type=MESH,
         )
 
+    mask[0] = (1 << rounds[0]) | (1 << rounds[1]) | (1 << rounds[2])
     barrier = pltpu.get_barrier_semaphore()
     for other in range(1, N_CTX):
         pl.semaphore_signal(
@@ -238,18 +366,20 @@
         copy.wait_send()
 
 
-def local_gradient(hidden, queries, values, cotangent, key_weight, doc_ids):
+def local_gradient(hidden, queries, values, cotangent, key_weight, doc_ids, round_index):
     depth = hidden.shape[1]
     dma = pltpu.SemaphoreType.DMA
     bf16, f32 = jnp.bfloat16, jnp.float32
-    any_spec = pl.BlockSpec(memory_space=pl.ANY)
+    hbm = pl.BlockSpec(memory_space=pltpu.HBM)
+    smem = pl.BlockSpec(memory_space=pltpu.SMEM)
     vmem = pl.BlockSpec(memory_space=pltpu.VMEM)
     seq = N_CTX * ROWS
     return pl.pallas_call(
         gradient_kernel,
-        out_shape=[jax.ShapeDtypeStruct((depth, 128), bf16)] * 2,
-        in_specs=[any_spec] * 5 + [vmem],
-        out_specs=[vmem] * 2,
+        out_shape=[jax.ShapeDtypeStruct((depth, 128), bf16)] * 2
+        + [jax.ShapeDtypeStruct((1,), jnp.int32)],
+        in_specs=[hbm] * 5 + [vmem, smem],
+        out_specs=[vmem, vmem, smem],
         scratch_shapes=[
             pltpu.VMEM((N_CTX, ROWS, depth), bf16),
             pltpu.VMEM((N_CTX, ROWS, HDIM), bf16),
@@ -282,19 +412,14 @@
             collective_id=0, has_side_effects=True, vmem_limit_bytes=48 * 1024 * 1024
         ),
         name="gradient",
-    )(hidden, queries, values, cotangent, key_weight, doc_ids)
+    )(hidden, queries, values, cotangent, key_weight, doc_ids, round_index)
 
 
 def on_device(hidden, queries, values, cotangent, key_weight, doc_ids, round_index):
-    rounds = lax.axis_size("rep").bit_length() - 1
-    gradient, averaged = local_gradient(
-        hidden[0], queries[0], values[0], cotangent[0], key_weight[0], doc_ids
+    gradient, stepped, mask = local_gradient(
+        hidden[0], queries[0], values[0], cotangent[0], key_weight[0], doc_ids, round_index
     )
-    for turn in range(GOSSIP):
-        partner = round_partner(averaged, round_index[turn], rounds)
-        averaged = (0.5 * (averaged.astype(jnp.float32) + partner.astype(jnp.float32))).astype(
-            jnp.bfloat16
-        )
+    averaged = gossip_rounds(stepped, mask[0])
     return (averaged[None], gradient[None])
 
 

time: 241 us -> 166 us (0.69)
  the two profiles are of different devices: /device:TPU:60 before, /device:TPU:64 now
where the time goes in v1:
time: 166 us; the launch traced here: 165 us
  Pallas kernels  156 us (94%)
  local copies, waits for them, and re-layouts  7.89 us (5%)
    pallas_call x1, Pallas kernels, local_gradient(): pl.pallas_call(gradient_kernel, out_shape=[jax.ShapeDtypeStruct((depth, 1...  113 us
    pallas_call x1, Pallas kernels, run(): pl.pallas_call(partial(gossip_kernel, bits), out_shape=jax.ShapeDtypeStru...  42.5 us
    unnamed x16, local copies, waits for them, and re-layouts  7.89 us

profile of v1, /device:TPU:64, one launch (start us, length us, event | category | flops | bytes accessed | tf_op | source)
XLA Modules:
  0.0 165.3 jit_solution(822554129329825874)
XLA Ops:
  0.6 0.0 copy-start.5
  0.6 0.0 copy-start.6
  0.7 0.6 copy-done.5
  1.3 0.0 copy-done.6
  1.3 0.0 copy-start
  1.3 1.2 copy-done
  2.5 0.0 copy-start.1
  2.5 1.2 copy-done.1
  3.7 0.0 copy-start.2
  3.7 1.0 copy-done.2
  4.7 0.0 copy-start.3
  4.7 1.0 copy-done.3
  5.7 0.0 copy-start.4
  5.7 0.9 copy-done.4
  6.7 113.1 %gradient.1 = (bf16[3584,128]{1,0:T(8,128)(2,1)S(1)}, bf16[3584,128]{1,0:T(8,128)(2,1)S(1)}, s32[1]{0:T(128)}) custom-call(bf16[128,3584]{1,0:T(8,128)(2,1)S(1)} %bitcast.9, bf16[128,2048]{1,0:T(8,128)(2,1)S(1)} %bitcast.11, bf16[128,1024]{1,0:T(8,128)(2,1)S(1)} %bitcast.13, bf16[128,2048]{1,0:T(8,128)(2,1)S(1)} %bitcast.12, bf16[3584,128]{1,0:T(8,128)(2,1)S(1)} %bitcast.10, ...), custom_call_target="tpu_custom_call" | custom-call | tf_op jit(solution)/shard_map/gradient/pallas_call | solution.py:377
  120.5 43.0 %conditional.1 = (bf16[3584,128]{1,0:T(8,128)(2,1)S(1)}) conditional(s32[]{:T(128)} %bitcast.5, bf16[3584,128]{1,0:T(8,128)(2,1)S(1)} %get-tuple-element.185, bf16[3584,128]{1,0:T(8,128)(2,1)S(1)} %get-tuple-element.185, bf16[3584,128]{1,0:T(8,128)(2,1)S(1)} %get-tuple-element.185, ...), branch_computations={%region_0.0_spmd, %region_1.0_spmd, %region_2.0_spmd, %region_3.0_... | conditional | bytes 1835016 | solution.py:158
  120.7 42.5 %gossip.57 = bf16[3584,128]{1,0:T(8,128)(2,1)S(1)} custom-call(bf16[3584,128]{1,0:T(8,128)(2,1)S(1)} %x.16), custom_call_target="tpu_custom_call" | custom-call | tf_op jit(solution)/shard_map/cond/branch_18_fun/gossip/pallas_call | solution.py:134
  163.5 0.9 copy.75
  164.4 0.9 copy.76
Async XLA Ops:
  0.6 0.7 copy-start.5
  0.6 0.7 copy-start.6
  1.3 1.2 copy-start
  2.5 1.2 copy-start.1
  3.7 1.0 copy-start.2
  4.7 1.0 copy-start.3
  5.7 0.9 copy-start.4
